TPU v7x, 32 devices: a whole 2x2x4 slice. The times are simulated.
32 devices in a mesh: groups: 2 (over y), req: 4 (over x, core), tensor: 4 (over z).
Axes of the slice: x: 2, y: 2, z: 4, core: 2. Of those that a mesh axis runs over, the one named last changes fastest.
Arguments:
- hidden: bfloat16 [384, 24576], P(('groups', 'req'), 'tensor'), parts along dimension 0, may hold values from -6 to 6
- join_weight: bfloat16 [24576, 8192], P('tensor', 'req'), may hold values from -0.0390625 to 0.0390625
- norm_gain: bfloat16 [8192], P(('req', 'tensor')), may hold values from 0.099609375 to 1.8984375
- qkv_weight: bfloat16 [8192, 9216], P(('req', 'tensor')), may hold values from -0.0625 to 0.0625
- owner_draft_cache: bfloat16 [48, 512, 2, 512], P(('groups', 'req'), 'tensor'), parts along dimension 0, may hold values from -250 to 250
- node_count: int32 [48], P('groups'), parts along dimension 0, may hold values from 1 to 8, as said below
- owner: int32 [48], P('groups'), parts along dimension 0, may hold values from 0 to 3, as said below
- cache_len: int32 [48], P('groups'), parts along dimension 0, may hold values from 1 to 512, as said below
Outputs:
- draft_attention: bfloat16 [48, 8, 8192], P(('groups', 'req'), None, 'tensor'), parts along dimension 0
There are 2 independent parts, one for each index of `groups`. A program takes and returns all parts, laid end to end along the dimension named above; an argument that names none is the same for every part. Nothing has to cross between parts.
Inputs may be any that keep to these rules, and one draw needn't show every extreme that they name: Every owner holds exactly 6 requests. `node_count`: some request has all 8 nodes live. `cache_len`: some slot uses all 512 positions.
All inputs are finite; a program needn't handle non-finite values.
Results may differ from a plain program's by a relative error of at most 0.01655.
The roundings to bfloat16 on the way count: a program that leaves them out, or rounds other values in their place, can miss the bound.
Values may be sent and summed in bfloat16 or wider, within the bound.
A program may use at most 256 MiB of HBM per device.

v0:
```python
import jax
import jax.numpy as jnp
from jax import lax
from jax.sharding import PartitionSpec as P

DF = 8192
QUERY_HEADS = 64
KEY_VALUE_HEADS = 4
HEAD_SIZE = 128
TREE_SLOTS = 8
CACHE_BLOCK = 128


norm_eps = 1e-05


def body(
    hidden, join_weight, norm_gain, qkv_weight, owner_draft_cache, node_count, owner, cache_len
):
    req_count = lax.axis_size("req")
    tensor_count = lax.axis_size("tensor")
    req_here = lax.axis_index("req")
    tensor_here = lax.axis_index("tensor")
    request_per_owner = owner_draft_cache.shape[0]
    count_all = owner.shape[0]
    piece_width = join_weight.shape[1] // tensor_count
    local_rows = request_per_owner * TREE_SLOTS
    same_owner = owner[:, None] == owner[None, :]
    earlier = jnp.arange(count_all)[None, :] < jnp.arange(count_all)[:, None]
    ranking = jnp.sum((same_owner & earlier).astype(jnp.int32), axis=1)
    slot_of = owner * request_per_owner + ranking
    slot_table = slot_of[None, :] == jnp.arange(count_all, dtype=jnp.int32)[:, None]
    partial_sum = jnp.dot(
        hidden,
        lax.all_gather(join_weight, "req", axis=1, tiled=True),
        preferred_element_type=jnp.float32,
    )
    partial_sum = partial_sum.reshape(local_rows, req_count, tensor_count, piece_width)
    own_joined = lax.psum_scatter(partial_sum, "tensor", scatter_dimension=2, tiled=True).astype(
        jnp.bfloat16
    )
    own_joined = own_joined.reshape(request_per_owner, TREE_SLOTS * req_count * piece_width)
    local_slots = lax.dynamic_slice_in_dim(slot_of, req_here * request_per_owner, request_per_owner)
    route_table = (jnp.arange(count_all, dtype=jnp.int32)[:, None] == local_slots[None, :]).astype(
        jnp.bfloat16
    )
    send_rows = jnp.dot(route_table, own_joined, preferred_element_type=jnp.float32).astype(
        jnp.bfloat16
    )
    send_rows = send_rows.reshape(
        req_count, request_per_owner, TREE_SLOTS * req_count * piece_width
    )
    arrived = lax.all_to_all(send_rows, "req", split_axis=0, concat_axis=0, tiled=True)
    joined = jnp.sum(arrived.astype(jnp.float32), axis=0).astype(jnp.bfloat16)
    joined = joined.reshape(local_rows, req_count * piece_width)
    projection, gain_part = (
        lax.all_gather(qkv_weight, "req", axis=0, tiled=True),
        lax.all_gather(norm_gain, "req", axis=0, tiled=True),
    )
    widened = joined.astype(jnp.float32)
    scaled = (widened * gain_part.astype(jnp.float32)).astype(jnp.bfloat16)
    partial_qkv = jnp.dot(scaled, projection, preferred_element_type=jnp.float32)
    row_squares = jnp.sum(widened * widened, axis=1)
    total_qkv, total_squares = lax.psum((partial_qkv, row_squares), "tensor")
    query_key_value = (total_qkv * lax.rsqrt(total_squares[:, None] / DF + norm_eps)).astype(
        jnp.bfloat16
    )
    query_group_width = QUERY_HEADS // KEY_VALUE_HEADS
    query_rows = query_key_value[:, : QUERY_HEADS * HEAD_SIZE].reshape(
        request_per_owner, TREE_SLOTS, KEY_VALUE_HEADS, query_group_width, HEAD_SIZE
    )
    fresh_key = query_key_value[
        :, QUERY_HEADS * HEAD_SIZE : (QUERY_HEADS + KEY_VALUE_HEADS) * HEAD_SIZE
    ].reshape(request_per_owner, TREE_SLOTS, KEY_VALUE_HEADS, HEAD_SIZE)
    fresh_value = query_key_value[:, (QUERY_HEADS + KEY_VALUE_HEADS) * HEAD_SIZE :].reshape(
        request_per_owner, TREE_SLOTS, KEY_VALUE_HEADS, HEAD_SIZE
    )
    cached_key_rows = owner_draft_cache[:, :, 0].reshape(
        request_per_owner, CACHE_BLOCK, KEY_VALUE_HEADS, HEAD_SIZE
    )
    cached_value_rows = owner_draft_cache[:, :, 1].reshape(
        request_per_owner, CACHE_BLOCK, KEY_VALUE_HEADS, HEAD_SIZE
    )
    lengths = lax.dynamic_slice_in_dim(cache_len, req_here * request_per_owner, request_per_owner)
    live_all = jnp.sum(jnp.where(slot_table, node_count[None, :], 0), axis=1)
    live_slot = lax.dynamic_slice_in_dim(live_all, req_here * request_per_owner, request_per_owner)
    scale_factor = HEAD_SIZE ** (-0.5)
    positions = tensor_here * CACHE_BLOCK + jnp.arange(CACHE_BLOCK)
    cache_mask = (positions[None, :] < lengths[:, None])[:, None, None, None, :]
    score_cache = (
        jnp.einsum(
            "snkgd,spkd->snkgp", query_rows, cached_key_rows, preferred_element_type=jnp.float32
        )
        * scale_factor
    )
    score_cache = jnp.where(cache_mask, score_cache, -1e30)
    first_block = tensor_here == 0
    new_mask = (jnp.arange(TREE_SLOTS)[None, :] <= jnp.arange(TREE_SLOTS)[:, None]) & first_block
    new_mask = new_mask[None, :, None, None, :]
    score_new = (
        jnp.einsum("snkgd,smkd->snkgm", query_rows, fresh_key, preferred_element_type=jnp.float32)
        * scale_factor
    )
    score_new = jnp.where(new_mask, score_new, -1e30)
    local_top = jnp.maximum(jnp.max(score_cache, axis=-1), jnp.max(score_new, axis=-1))
    top_score = lax.pmax(local_top, "tensor")
    weight_cache = jnp.where(cache_mask, jnp.exp(score_cache - top_score[..., None]), 0.0)
    weight_new = jnp.where(new_mask, jnp.exp(score_new - top_score[..., None]), 0.0)
    denominator = jnp.sum(weight_cache, axis=-1) + jnp.sum(weight_new, axis=-1)
    accum = jnp.einsum(
        "snkgp,spkd->snkgd",
        weight_cache.astype(jnp.bfloat16),
        cached_value_rows,
        preferred_element_type=jnp.float32,
    )
    accum = accum + jnp.einsum(
        "snkgm,smkd->snkgd",
        weight_new.astype(jnp.bfloat16),
        fresh_value,
        preferred_element_type=jnp.float32,
    )
    head_cols = QUERY_HEADS * HEAD_SIZE // tensor_count
    accum_all, denom_all = lax.psum((accum, denominator), "tensor")
    result_all = (accum_all / denom_all[..., None]).reshape(
        request_per_owner, TREE_SLOTS, QUERY_HEADS * HEAD_SIZE
    )
    result = lax.dynamic_slice_in_dim(result_all, tensor_here * head_cols, head_cols, 2)
    alive = (jnp.arange(TREE_SLOTS)[None, :] < live_slot[:, None])[:, :, None]
    return jnp.where(alive, result, 0.0).astype(jnp.bfloat16)


def solution(mesh):
    return jax.shard_map(
        body,
        mesh=mesh,
        in_specs=(
            P(("groups", "req"), "tensor"),
            P("tensor", "req"),
            P(("req", "tensor")),
            P(("req", "tensor"), None),
            P(("groups", "req"), "tensor", None, None),
            P("groups"),
            P("groups"),
            P("groups"),
        ),
        out_specs=P(("groups", "req"), None, "tensor"),
        check_vma=False,
    )
```

profile of v0, /device:TPU:0, one launch (start us, length us, event | category | flops | bytes accessed | tf_op | source)
XLA Modules:
  0.0 1098.4 jit_solution(17785400994742120650)
XLA Ops:
  7.3 588.3 %all-gather.4.cloned.1.call-done = bf16[6144,8192]{1,0:T(8,128)(2,1)} async-done(((bf16[6144,2048]{1,0:T(8,128)(2,1)}), bf16[6144,8192]{1,0:T(8,128)(2,1)}) %all-gather.4.cloned.1.call-update) | async-done | bytes 100663312 | tf_op jit(solution)/shard_map/all_gather | solution.py:35
  595.6 34.8 %fusion.28 = f32[48,8192]{1,0:T(8,128)S(1)} fusion(bf16[48,6144]{1,0:T(8,128)(2,1)S(1)} %copy-done, bf16[6144,8192]{1,0:T(8,128)(2,1)} %all-gather.4.cloned.1.call-done), kind=kOutput, calls=%fused_computation.51 | convolution fusion | flops 4831838208 | bytes 102825984 | tf_op jit(solution)/shard_map/dot_general | solution.py:33
  630.4 2.2 reshape.97
  632.6 3.5 copy.28
  637.1 34.5 %reduce-scatter.2.cloned.1.call-done = f32[48,4,1,512]{3,0,1,2:T(8,128)} async-done(((f32[48,4,4,512]{3,0,1,2:T(8,128)}), f32[48,4,1,512]{3,0,1,2:T(8,128)}) %reduce-scatter.2.cloned.1.call-update) | async-done | bytes 393232 | tf_op jit(solution)/shard_map/reduce_scatter | solution.py:39
  671.6 1.0 convert_element_type.37
  673.3 1.3 reshape.99
  674.5 3.5 all-to-all-start
  678.1 15.3 %all-gather = bf16[4,1,512]{2,1,0:T(2,128)(2,1)S(1)} all-gather(bf16[1,1,512]{2,1,0:T(2,128)(2,1)S(1)} %reshape.105), channel_id=1, replica_groups=mesh['groups'=2,'req'=4,'tensor'=4] {'req'}, dimensions={0}, use_global_device_ids=true | all-gather | bytes 5120 | tf_op jit(solution)/shard_map/all_gather | solution.py:58
  694.1 205.3 %all-gather.6.cloned.1.call-done = bf16[2048,9216]{1,0:T(8,128)(2,1)} async-done(((bf16[512,9216]{1,0:T(8,128)(2,1)}), bf16[2048,9216]{1,0:T(8,128)(2,1)}) %all-gather.6.cloned.1.call-update) | async-done | bytes 37748752 | tf_op jit(solution)/shard_map/all_gather | solution.py:57
  899.4 16.3 %fusion.19 = f32[48,9216]{1,0:T(8,128)} fusion(bf16[2048,9216]{1,0:T(8,128)(2,1)} %all-gather.6.cloned.1.call-done, f32[48,2048]{1,0:T(8,128)S(1)} %reshape.104, f32[2048]{0:T(1024)S(1)} %bitcast.62), kind=kOutput, calls=%fused_computation.29 | convolution fusion | flops 1812135936 | bytes 39919616 | tf_op jit(solution)/shard_map/dot_general | solution.py:62
  917.1 3.4 fusion.26
  920.6 4.8 copy.45
  925.4 2.6 copy.46
  928.2 12.6 %psum.29 = f32[48]{0:T(128)S(1)} all-reduce(f32[48]{0:T(128)S(1)} %multiply_reduce_fusion), channel_id=1, replica_groups=mesh['groups'=2,'req'=4,'tensor'=4] {'tensor'}, use_global_device_ids=true, to_apply=%region_6.7 | all-reduce | flops 48 | bytes 384 | tf_op jit(solution)/shard_map/psum | solution.py:64
  940.8 50.9 %all-reduce.3.cloned.1.call-done = f32[48,9216]{1,0:T(8,128)} async-done(((f32[48,9216]{1,0:T(8,128)}), f32[48,9216]{1,0:T(8,128)}) %all-reduce.3.cloned.1.call-update) | async-done | bytes 1769488 | tf_op jit(solution)/shard_map/psum | solution.py:64
  991.7 1.6 multiply_convert_fusion
  993.4 2.0 fusion.27
  996.1 18.5 %pmax.7 = f32[6,8,4,16]{3,1,2,0:T(8,128)S(1)} all-reduce(f32[6,8,4,16]{3,1,2,0:T(8,128)S(1)} %max.5), channel_id=1, replica_groups=mesh['groups'=2,'req'=4,'tensor'=4] {'tensor'}, use_global_device_ids=true, to_apply=%region_9.10 | all-reduce | flops 3072 | bytes 24576 | tf_op jit(solution)/shard_map/pmax | solution.py:106
  1014.5 1.7 fusion.6
  1016.3 2.6 bitcast_add_fusion
  1021.1 21.0 %psum.31 = f32[6,8,4,16]{3,1,2,0:T(8,128)S(1)} all-reduce(f32[6,8,4,16]{3,1,2,0:T(8,128)S(1)} %add.51), channel_id=1, replica_groups=mesh['groups'=2,'req'=4,'tensor'=4] {'tensor'}, use_global_device_ids=true, to_apply=%region_13.14 | all-reduce | flops 3072 | bytes 24576 | tf_op jit(solution)/shard_map/psum | solution.py:123
  1042.1 46.5 %all-reduce.5.cloned.1.call-done = f32[6,8,4,16,128]{4,3,1,2,0:T(8,128)} async-done(((f32[6,8,4,16,128]{4,3,1,2,0:T(8,128)}), f32[6,8,4,16,128]{4,3,1,2,0:T(8,128)}) %all-reduce.5.cloned.1.call-update) | async-done | bytes 1572880 | tf_op jit(solution)/shard_map/psum | solution.py:123
  1088.6 1.9 broadcast_divide_fusion
  (59 shorter events, 9.0 us)
Async XLA Ops:
  6.5 589.1 %copy-start = (bf16[48,6144]{1,0:T(8,128)(2,1)S(1)}, bf16[48,6144]{1,0:T(8,128)(2,1)}, u32[]{:S(2)}) copy-start(bf16[48,6144]{1,0:T(8,128)(2,1)} %param.8) | copy-start | bytes 1769476
  6.5 589.1 %all-gather.4.cloned.1.call-start = ((), (), s32[]{:S(2)}) async-start(), calls=%async_computation.2 | async-start | bytes 125829120 | tf_op jit(solution)/shard_map/all_gather | solution.py:35
  7.3 664.3 %reduce-scatter.2.cloned.1.call-start = ((), (), s32[]{:S(2)}) async-start(), calls=%async_computation.3 | async-start | bytes 1966080 | tf_op jit(solution)/shard_map/reduce_scatter | solution.py:39
  636.1 0.8 copy-start.7
  636.1 263.3 %all-gather.6.cloned.1.call-start = ((), (), s32[]{:S(2)}) async-start(), calls=%async_computation.4 | async-start | bytes 47185920 | tf_op jit(solution)/shard_map/all_gather | solution.py:57
  673.3 4.8 copy-start.6
  674.5 18.9 %all-to-all-start = ((bf16[4,6,16384]{2,1,0:T(8,128)(2,1)}), bf16[4,6,16384]{2,1,0:T(8,128)(2,1)S(1)}, u32[]{:S(2)}, u32[]{:S(2)}) async-start(bf16[4,6,16384]{2,1,0:T(8,128)(2,1)} %reshape.99), calls=%async_computation.1 | async-start | bytes 2097152 | tf_op jit(solution)/shard_map/all_to_all | solution.py:53
  678.1 313.6 %all-reduce.3.cloned.1.call-start = ((), (), s32[]{:S(2)}) async-start(), calls=%async_computation.5 | async-start | bytes 3538944 | tf_op jit(solution)/shard_map/psum | solution.py:64
  915.7 0.7 copy-start.8
  915.7 1.4 copy-start.2
  915.7 172.8 %all-reduce.5.cloned.1.call-start = ((), (), s32[]{:S(2)}) async-start(), calls=%async_computation.6 | async-start | bytes 3145728 | tf_op jit(solution)/shard_map/psum | solution.py:123
  920.6 4.8 copy-start.3
  993.3 2.0 copy-start.4
  993.3 2.0 copy-start.5
  1018.9 0.7 copy-start.9
  1088.6 3.3 copy-start.1
Sparse Core Ops, SparseCore 0:
  8.9 586.6 all-gather.3
  636.2 35.3 reduce-scatter.1
  673.2 226.1 all-gather.5
  915.9 75.7 all-reduce.2
  1019.0 69.5 all-reduce.4
where the time goes:
time: 1100 us
  waiting for transfers between devices  927 us (84%)
  blocking collectives  67.4 us (6%)
  matrix products  58.3 us (5%)
  local copies, waits for them, and re-layouts  21.2 us (2%)
  between operations  13.4 us (1%)
    all_gather x1, waiting for transfers between devices, body(): lax.all_gather(join_weight, 'req', axis=1, tiled=True)  588 us
    all_gather x1, waiting for transfers between devices, body(): lax.all_gather(qkv_weight, 'req', axis=0, tiled=True)  205 us
    psum x1, waiting for transfers between devices, body(): total_qkv, total_squares = lax.psum((partial_qkv, row_squares), 'tensor')  50.9 us
    psum x1, waiting for transfers between devices, body(): accum_all, denom_all = lax.psum((accum, denominator), 'tensor')  46.5 us
    dot_general x1, matrix products, body(): jnp.dot(hidden, lax.all_gather(join_weight, 'req', axis=1, tiled=True), p...  34.8 us
    reduce_scatter x1, waiting for transfers between devices, body(): lax.psum_scatter(partial_sum, 'tensor', scatter_dimension=2, tiled=True)  34.5 us
  transfers between devices with their start and end apart: 6, of which 5 were waited for; matrix products, arithmetic and copies ran while one was open for 2% of the time, Pallas kernels for 0%

commit v1 on v0

--- a/solution.py
+++ b/solution.py
@@ -14,54 +14,46 @@
 norm_eps = 1e-05
 
 
+def slots(owner, request_per_owner):
+    count_all = owner.shape[0]
+    same_owner = owner[:, None] == owner[None, :]
+    earlier = jnp.arange(count_all)[None, :] < jnp.arange(count_all)[:, None]
+    ranking = jnp.sum((same_owner & earlier).astype(jnp.int32), axis=1)
+    return owner * request_per_owner + ranking
+
+
 def body(
     hidden, join_weight, norm_gain, qkv_weight, owner_draft_cache, node_count, owner, cache_len
 ):
-    req_count = lax.axis_size("req")
     tensor_count = lax.axis_size("tensor")
     req_here = lax.axis_index("req")
     tensor_here = lax.axis_index("tensor")
     request_per_owner = owner_draft_cache.shape[0]
     count_all = owner.shape[0]
-    piece_width = join_weight.shape[1] // tensor_count
-    local_rows = request_per_owner * TREE_SLOTS
-    same_owner = owner[:, None] == owner[None, :]
-    earlier = jnp.arange(count_all)[None, :] < jnp.arange(count_all)[:, None]
-    ranking = jnp.sum((same_owner & earlier).astype(jnp.int32), axis=1)
-    slot_of = owner * request_per_owner + ranking
+    slot_of = slots(owner, request_per_owner)
     slot_table = slot_of[None, :] == jnp.arange(count_all, dtype=jnp.int32)[:, None]
-    partial_sum = jnp.dot(
-        hidden,
-        lax.all_gather(join_weight, "req", axis=1, tiled=True),
-        preferred_element_type=jnp.float32,
-    )
-    partial_sum = partial_sum.reshape(local_rows, req_count, tensor_count, piece_width)
-    own_joined = lax.psum_scatter(partial_sum, "tensor", scatter_dimension=2, tiled=True).astype(
+    rows_all = count_all * TREE_SLOTS
+    hidden_all = lax.all_gather(hidden, "req", axis=0, tiled=True)
+    partial_sum = jnp.dot(hidden_all, join_weight, preferred_element_type=jnp.float32)
+    joined = lax.psum_scatter(partial_sum, "tensor", scatter_dimension=1, tiled=True).astype(
         jnp.bfloat16
     )
-    own_joined = own_joined.reshape(request_per_owner, TREE_SLOTS * req_count * piece_width)
-    local_slots = lax.dynamic_slice_in_dim(slot_of, req_here * request_per_owner, request_per_owner)
-    route_table = (jnp.arange(count_all, dtype=jnp.int32)[:, None] == local_slots[None, :]).astype(
-        jnp.bfloat16
+    features = joined.shape[1]
+    joined = jnp.dot(
+        slot_table.astype(jnp.bfloat16),
+        joined.reshape(count_all, TREE_SLOTS * features),
+        preferred_element_type=jnp.float32,
+    ).reshape(rows_all, features)
+    scaled = (joined * norm_gain.astype(jnp.float32)).astype(jnp.bfloat16)
+    partial_qkv = jnp.dot(scaled, qkv_weight, preferred_element_type=jnp.float32)
+    row_squares = jnp.sum(joined * joined, axis=1)
+    own_qkv = lax.psum_scatter(partial_qkv, "req", scatter_dimension=0, tiled=True)
+    total_squares = lax.dynamic_slice_in_dim(
+        lax.psum(row_squares, ("req", "tensor")),
+        req_here * request_per_owner * TREE_SLOTS,
+        request_per_owner * TREE_SLOTS,
     )
-    send_rows = jnp.dot(route_table, own_joined, preferred_element_type=jnp.float32).astype(
-        jnp.bfloat16
-    )
-    send_rows = send_rows.reshape(
-        req_count, request_per_owner, TREE_SLOTS * req_count * piece_width
-    )
-    arrived = lax.all_to_all(send_rows, "req", split_axis=0, concat_axis=0, tiled=True)
-    joined = jnp.sum(arrived.astype(jnp.float32), axis=0).astype(jnp.bfloat16)
-    joined = joined.reshape(local_rows, req_count * piece_width)
-    projection, gain_part = (
-        lax.all_gather(qkv_weight, "req", axis=0, tiled=True),
-        lax.all_gather(norm_gain, "req", axis=0, tiled=True),
-    )
-    widened = joined.astype(jnp.float32)
-    scaled = (widened * gain_part.astype(jnp.float32)).astype(jnp.bfloat16)
-    partial_qkv = jnp.dot(scaled, projection, preferred_element_type=jnp.float32)
-    row_squares = jnp.sum(widened * widened, axis=1)
-    total_qkv, total_squares = lax.psum((partial_qkv, row_squares), "tensor")
+    total_qkv = lax.psum(own_qkv, "tensor")
     query_key_value = (total_qkv * lax.rsqrt(total_squares[:, None] / DF + norm_eps)).astype(
         jnp.bfloat16
     )

time: 1100 us -> 342 us (0.31)
  waiting for transfers between devices: 927 us -> 207 us
  matrix products: 58.3 us -> 27.2 us
    all_gather x2 -> x1, waiting for transfers between devices: 794 us -> 28.4 us  [body(): hidden_all = lax.all_gather(hidden, 'req', axis=0, tiled=True)]
    reduce_scatter x1 -> x2, waiting for transfers between devices: 34.5 us -> 97.3 us  [the longest x1 62.7 us: body(): lax.psum_scatter(partial_qkv, 'req', scatter_dimension=0, tiled=True)]
    dot_general x3, matrix products: 51.4 us -> 21.1 us  [the longest x1 12.3 us: body(): jnp.dot(hidden_all, join_weight, preferred_element_type=jnp.float32)]
    psum x1, blocking collectives: 12.6 us -> 34.1 us  [body(): lax.psum(row_squares, ('req', 'tensor'))]
    psum x1, waiting for transfers between devices: 50.9 us -> 34.3 us  [body(): total_qkv = lax.psum(own_qkv, 'tensor')]
    all_gather x1 -> x0, blocking collectives: 15.3 us -> none  [body(): lax.all_gather(norm_gain, 'req', axis=0, tiled=True)]
  transfers between devices with their start and end apart: 6 -> 5, of which waited for: 5 -> 5; matrix products, arithmetic and copies ran while one was open for 2% -> 4% of each run, Pallas kernels for 0% -> 0%
where the time goes in v1:
time: 342 us; the launch traced here: 341 us
  waiting for transfers between devices  207 us (61%)
  blocking collectives  73.6 us (22%)
  matrix products  27.2 us (8%)
  between operations  13.3 us (4%)
  local copies, waits for them, and re-layouts  12.5 us (4%)
  other arithmetic  7.31 us (2%)
    reduce_scatter x1, waiting for transfers between devices, body(): lax.psum_scatter(partial_qkv, 'req', scatter_dimension=0, tiled=True)  62.7 us
    psum x1, waiting for transfers between devices, body(): accum_all, denom_all = lax.psum((accum, denominator), 'tensor')  46.5 us
    reduce_scatter x1, waiting for transfers between devices, body(): lax.psum_scatter(partial_sum, 'tensor', scatter_dimension=1, tiled=True)  34.6 us
    psum x1, waiting for transfers between devices, body(): total_qkv = lax.psum(own_qkv, 'tensor')  34.3 us
    psum x1, blocking collectives, body(): lax.psum(row_squares, ('req', 'tensor'))  34.1 us
    all_gather x1, waiting for transfers between devices, body(): hidden_all = lax.all_gather(hidden, 'req', axis=0, tiled=True)  28.4 us
    psum x1, blocking collectives, body(): accum_all, denom_all = lax.psum((accum, denominator), 'tensor')  21 us
    pmax x1, blocking collectives, body(): top_score = lax.pmax(local_top, 'tensor')  18.5 us
  transfers between devices with their start and end apart: 5, of which 5 were waited for; matrix products, arithmetic and copies ran while one was open for 4% of the time, Pallas kernels for 0%

profile of v1, /device:TPU:0, one launch (start us, length us, event | category | flops | bytes accessed | tf_op | source)
XLA Modules:
  0.0 341.3 jit_solution(7624498871045635591)
XLA Ops:
  6.5 0.7 all-gather.2.cloned.1.call-update
  7.3 28.4 %all-gather.2.cloned.1.call-done = bf16[192,6144]{1,0:T(8,128)(2,1)} async-done(((bf16[48,6144]{1,0:T(8,128)(2,1)}), bf16[192,6144]{1,0:T(8,128)(2,1)}) %all-gather.2.cloned.1.call-update) | async-done | bytes 2359312 | tf_op jit(solution)/shard_map/all_gather | solution.py:36
  35.7 12.3 %fusion.29 = f32[192,2048]{1,0:T(8,128)} fusion(bf16[192,6144]{1,0:T(8,128)(2,1)} %all-gather.2.cloned.1.call-done, bf16[6144,2048]{1,0:T(8,128)(2,1)} %param.9), kind=kOutput, calls=%fused_computation.50 | convolution fusion | flops 4831838208 | bytes 29097984 | tf_op jit(solution)/shard_map/dot_general | solution.py:37
  48.9 34.6 %reduce-scatter.3.cloned.1.call-done = f32[192,512]{1,0:T(8,128)} async-done(((f32[192,2048]{1,0:T(8,128)}), f32[192,512]{1,0:T(8,128)}) %reduce-scatter.3.cloned.1.call-update) | async-done | bytes 393232 | tf_op jit(solution)/shard_map/reduce_scatter | solution.py:38
  83.5 1.0 convert_element_type.26
  84.9 8.6 %fusion.19 = f32[192,9216]{1,0:T(8,128)} fusion(bf16[512,9216]{1,0:T(8,128)(2,1)} %param.11, f32[192,512]{1,0:T(8,128)S(1)} %reshape.91, f32[512]{0:T(512)S(1)} %convert_element_type.27), kind=kOutput, calls=%fused_computation.28 | convolution fusion | flops 1812135936 | bytes 16910336 | tf_op jit(solution)/shard_map/dot_general | solution.py:48
  93.6 62.7 %reduce-scatter.5.cloned.1.call-done = f32[48,9216]{1,0:T(8,128)} async-done(((f32[192,9216]{1,0:T(8,128)}), f32[48,9216]{1,0:T(8,128)}) %reduce-scatter.5.cloned.1.call-update) | async-done | bytes 1769488 | tf_op jit(solution)/shard_map/reduce_scatter | solution.py:50
  156.4 3.1 fusion.27
  159.5 4.7 %copy.33 = bf16[6,128,1,512]{1,3,0,2:T(8,128)(2,1)} copy(bf16[6,128,1,512]{3,2,1,0:T(2,128)(2,1)} %get-tuple-element.5) | data formatting | bytes 1572864
  164.1 2.6 copy.34
  167.0 34.1 %psum.29 = f32[192]{0:T(256)S(1)} all-reduce(f32[192]{0:T(256)S(1)} %multiply_reduce_fusion), channel_id=1, replica_groups=mesh['groups'=2,'req'=4,'tensor'=4] {'req','tensor'}, use_global_device_ids=true, to_apply=%region_6.7 | all-reduce | flops 192 | bytes 1536 | tf_op jit(solution)/shard_map/psum | solution.py:52
  201.2 34.3 %all-reduce.3.cloned.1.call-done = f32[48,9216]{1,0:T(8,128)} async-done(((f32[48,9216]{1,0:T(8,128)}), f32[48,9216]{1,0:T(8,128)}) %all-reduce.3.cloned.1.call-update) | async-done | bytes 1769488 | tf_op jit(solution)/shard_map/psum | solution.py:56
  235.5 1.6 multiply_convert_fusion
  237.2 2.0 fusion.28
  239.1 0.6 bitcast_reduce_fusion
  239.8 18.5 %pmax.7 = f32[6,8,4,16]{3,1,2,0:T(8,128)S(1)} all-reduce(f32[6,8,4,16]{3,1,2,0:T(8,128)S(1)} %max.5), channel_id=1, replica_groups=mesh['groups'=2,'req'=4,'tensor'=4] {'tensor'}, use_global_device_ids=true, to_apply=%region_9.10 | all-reduce | flops 3072 | bytes 24576 | tf_op jit(solution)/shard_map/pmax | solution.py:98
  258.3 1.7 fusion.6
  260.0 1.8 bitcast_add_fusion
  261.8 0.6 copy-done.5
  263.1 0.9 fusion.4
  264.0 21.0 %psum.31 = f32[6,8,4,16]{3,1,2,0:T(8,128)S(1)} all-reduce(f32[6,8,4,16]{3,1,2,0:T(8,128)S(1)} %add.56), channel_id=1, replica_groups=mesh['groups'=2,'req'=4,'tensor'=4] {'tensor'}, use_global_device_ids=true, to_apply=%region_13.14 | all-reduce | flops 3072 | bytes 24576 | tf_op jit(solution)/shard_map/psum | solution.py:115
  285.0 46.5 %all-reduce.5.cloned.1.call-done = f32[6,8,4,16,128]{4,3,1,2,0:T(8,128)} async-done(((f32[6,8,4,16,128]{4,3,1,2,0:T(8,128)}), f32[6,8,4,16,128]{4,3,1,2,0:T(8,128)}) %all-reduce.5.cloned.1.call-update) | async-done | bytes 1572880 | tf_op jit(solution)/shard_map/psum | solution.py:115
  331.5 1.9 broadcast_divide_fusion
  334.0 0.8 select_convert_fusion
  (41 shorter events, 3.0 us)
Async XLA Ops:
  6.5 29.2 %all-gather.2.cloned.1.call-start = ((), (), s32[]{:S(2)}) async-start(), calls=%async_computation.2 | async-start | bytes 2949120 | tf_op jit(solution)/shard_map/all_gather | solution.py:36
  7.3 76.3 %reduce-scatter.3.cloned.1.call-start = ((), (), s32[]{:S(2)}) async-start(), calls=%async_computation.3 | async-start | bytes 1966080 | tf_op jit(solution)/shard_map/reduce_scatter | solution.py:38
  48.0 0.7 copy-start.2
  48.0 0.7 copy-start.3
  48.1 108.2 %reduce-scatter.5.cloned.1.call-start = ((), (), s32[]{:S(2)}) async-start(), calls=%async_computation.4 | async-start | bytes 8847360 | tf_op jit(solution)/shard_map/reduce_scatter | solution.py:50
  93.6 62.8 %copy-start = (bf16[6,128,2,512]{3,2,1,0:T(2,128)(2,1)S(1)}, bf16[6,128,2,512]{3,2,1,0:T(2,128)(2,1)}, u32[]{:S(2)}) copy-start(bf16[6,128,2,512]{3,2,1,0:T(2,128)(2,1)} %param.12) | copy-start | bytes 4718596
  93.6 141.9 %all-reduce.3.cloned.1.call-start = ((), (), s32[]{:S(2)}) async-start(), calls=%async_computation.5 | async-start | bytes 3538944 | tf_op jit(solution)/shard_map/psum | solution.py:56
  156.3 175.2 %all-reduce.5.cloned.1.call-start = ((), (), s32[]{:S(2)}) async-start(), calls=%async_computation.6 | async-start | bytes 3145728 | tf_op jit(solution)/shard_map/psum | solution.py:115
  164.1 2.6 copy-start.4
  237.1 2.0 copy-start.1
  261.8 0.7 copy-start.5
Sparse Core Ops, SparseCore 0:
  8.9 26.7 all-gather.1
  48.2 35.2 reduce-scatter.2
  93.7 62.5 reduce-scatter.4
  158.7 76.7 all-reduce.2
  261.9 69.5 all-reduce.4
